TPU v7x, 32 devices: a whole 2x2x4 slice. The times are simulated.
32 devices in a mesh: pipe: 8 (over z, x), tensor: 4 (over y, core).
Axes of the slice: x: 2, y: 2, z: 4, core: 2. Of those that a mesh axis runs over, the one named last changes fastest.
Arguments:
- section_weights: bfloat16 [8, 2, 4096, 4096], P('pipe', None, 'tensor'), may hold values from -0.09375 to 0.09375
- context: bfloat16 [8, 2, 768, 4096], P('pipe', None, None, 'tensor'), may hold values from -3 to 3
- grad_out: bfloat16 [8, 2, 768, 4096], P('pipe', None, 'tensor'), may hold values from -3 to 3
Outputs:
- weight_grad: bfloat16 [8, 4096, 4096], P('pipe', 'tensor')
- input_grad: bfloat16 [8, 2, 768, 4096], P('pipe', None, None, 'tensor')
All inputs are finite; a program needn't handle non-finite values.
Results may differ from a plain program's by a relative error of at most 0.001.
Values may be sent and summed in bfloat16 or wider, within the bound.
A program may use at most 192 MiB of HBM per device.

v0:
```python
import jax
import jax.numpy as jnp
from jax import lax
from jax.sharding import PartitionSpec as P


def from_behind(value, axis, by):
    count = lax.axis_size(axis)
    pairs = [(i, i + by) for i in range(count) if 0 <= i + by < count]
    return lax.ppermute(value, axis, pairs)


def shards(section_weights, context, grad_out):
    width_in = context.shape[3]
    width_out = grad_out.shape[3]
    owned = 2
    piece = lax.all_gather(grad_out, "tensor", axis=2, tiled=True)
    context_rows = context[0, :owned]
    weight_sum = jnp.einsum(
        "rtd,rto->rdo", context_rows, piece[0, :owned], preferred_element_type=jnp.float32
    )
    product = jnp.einsum(
        "rto,rdo->rtd", piece[0], section_weights[0], preferred_element_type=jnp.float32
    )
    back_rows = product
    weight_sum, back_rows = (weight_sum, back_rows)
    backward = back_rows.astype(jnp.bfloat16)
    from_next = from_behind(backward[0], "pipe", -1)
    from_prior = from_behind(backward[1], "pipe", 1)
    input_grad = jnp.stack([from_next, from_prior])[None]
    pieces = lax.axis_size("pipe")
    blocked = weight_sum[1].reshape(width_in, pieces, width_out // pieces)
    spread = lax.all_to_all(blocked, "pipe", split_axis=1, concat_axis=1, tiled=True)
    turned = spread[:, ::-1]
    partner = lax.all_to_all(turned, "pipe", split_axis=1, concat_axis=1, tiled=True).reshape(
        width_in, width_out
    )
    weight_grad = (weight_sum[0] + partner).astype(jnp.bfloat16)[None]
    return (weight_grad, input_grad)


def solution(mesh):
    placed = (
        P("pipe", None, "tensor", None),
        P("pipe", None, None, "tensor"),
        P("pipe", None, "tensor", None),
    )
    return jax.shard_map(
        shards,
        mesh=mesh,
        in_specs=placed,
        out_specs=(P("pipe", "tensor", None), P("pipe", None, None, "tensor")),
        check_vma=False,
    )
```

profile of v0, /device:TPU:17, one launch (start us, length us, event | category | flops | bytes accessed | tf_op | source)
XLA Modules:
  0.0 990.7 jit_solution(868376406514110776)
XLA Ops:
  7.2 0.0 copy-start
  7.2 0.0 all-gather.2.cloned.1.call-start
  7.2 0.7 all-gather.2.cloned.1.call-update
  7.9 85.3 %all-gather.2.cloned.1.call-done = bf16[1,2,768,4096]{3,2,1,0:T(8,128)(2,1)} async-done(((bf16[1,2,192,4096]{3,2,1,0:T(8,128)(2,1)}), bf16[1,2,768,4096]{3,2,1,0:T(8,128)(2,1)}) %all-gather.2.cloned.1.call-update) | async-done | bytes 12582928 | tf_op jit(solution)/shard_map/all_gather | solution.py:17
  93.2 0.0 copy-done
  93.2 22.0 %fusion.4 = f32[2,1024,4096]{2,1,0:T(8,128)} fusion(bf16[1,2,768,4096]{3,2,1,0:T(8,128)(2,1)} %all-gather.2.cloned.1.call-done, bf16[1,2,768,1024]{3,2,1,0:T(8,128)(2,1)S(1)} %copy-done), kind=kOutput, calls=%fused_computation.5 | convolution fusion | flops 12884901888 | bytes 49283072 | tf_op jit(solution)/shard_map/rtd,rto->rdo/dot_general | solution.py:19
  115.2 0.0 slice-start
  115.2 5.8 slice-done
  121.0 10.5 %copy.10 = f32[128,8,8,512]{3,2,1,0:T(8,128)S(1)} copy(f32[128,8,8,512]{3,1,2,0:T(8,128)S(1)} %bitcast.27) | data formatting | bytes 33554432
  131.5 19.0 %copy.7 = f32[1024,8,512]{2,0,1:T(8,128)S(1)} copy(f32[1024,8,512]{2,1,0:T(8,128)S(1)} %bitcast.26) | data formatting | bytes 33554432 | tf_op jit(solution)/shard_map/reshape;squeeze | solution.py:32
  150.5 366.6 %all_to_all.10 = f32[1024,8,512]{2,0,1:T(8,128)} all-to-all(f32[1024,8,512]{2,0,1:T(8,128)S(1)} %copy.7), channel_id=1, replica_groups=mesh['pipe'=8,'tensor'=4] {'pipe'}, dimensions={1} | all-to-all | bytes 33554432 | tf_op jit(solution)/shard_map/all_to_all | solution.py:33
  517.0 11.6 %rev.3 = f32[1024,8,512]{2,0,1:T(8,128)} reverse(f32[1024,8,512]{2,0,1:T(8,128)} %all_to_all.10), dimensions={1} | reverse | bytes 33554432 | tf_op jit(solution)/shard_map/rev | solution.py:34
  528.6 6.5 all-to-all-start.1
  535.1 18.6 %fusion.7 = bf16[2,768,1024]{2,1,0:T(8,128)(2,1)S(1)} fusion(bf16[1,2,1024,4096]{3,2,1,0:T(8,128)(2,1)} %param.3, bf16[1,2,768,4096]{3,2,1,0:T(8,128)(2,1)} %all-gather.2.cloned.1.call-done), kind=kOutput, calls=%fused_computation.9 | convolution fusion | flops 12886474752 | bytes 32505856 | tf_op jit(solution)/shard_map/rto,rdo->rtd/dot_general | solution.py:22
  553.7 0.3 slice_bitcast_fusion.1
  554.1 3.1 collective-permute-start
  557.2 2.4 collective-permute-start.1
  559.5 367.4 %collective-permute-done = bf16[768,1024]{1,0:T(8,128)(2,1)S(1)} collective-permute-done((bf16[768,1024]{1,0:T(8,128)(2,1)S(1)}, bf16[768,1024]{1,0:T(8,128)(2,1)S(1)}, u32[]{:S(2)}, u32[]{:S(2)}) %collective-permute-start) | collective-permute-done | bytes 1572896 | tf_op jit(solution)/shard_map/ppermute | solution.py:10
  927.0 4.0 collective-permute-done.1
  930.9 1.9 maximum_bitcast_fusion
  932.9 0.0 all-to-all-done.1
  932.9 17.7 %copy.8 = f32[1024,8,512]{2,1,0:T(8,128)} copy(f32[1024,8,512]{2,0,1:T(8,128)} %all-to-all-done.1) | data formatting | bytes 33554432 | tf_op jit(solution)/shard_map/all_to_all | solution.py:35
  950.6 0.0 copy-start.1
  950.6 18.3 %reshape.8 = f32[1,1024,4096]{2,1,0:T(8,128)} reshape(f32[1024,8,512]{2,1,0:T(8,128)} %copy.8) | data formatting | bytes 33554432 | tf_op jit(solution)/shard_map/reshape | solution.py:35
  968.9 14.9 %fusion = bf16[1,1024,4096]{2,1,0:T(8,128)(2,1)} fusion(f32[1,1024,4096]{2,1,0:T(8,128)} %reshape.8, f32[2,1024,4096]{2,1,0:T(8,128)} %fusion.4), kind=kLoop, calls=%fused_computation.1 | loop fusion | flops 8388608 | bytes 41943040 | tf_op jit(solution)/shard_map/convert_element_type | solution.py:38
  983.8 0.0 copy-done.1
Async XLA Ops:
  7.2 86.1 %copy-start = (bf16[1,2,768,1024]{3,2,1,0:T(8,128)(2,1)S(1)}, bf16[1,2,768,1024]{3,2,1,0:T(8,128)(2,1)}, u32[]{:S(2)}) copy-start(bf16[1,2,768,1024]{3,2,1,0:T(8,128)(2,1)} %param.4) | copy-start | bytes 9437188
  7.2 86.0 %all-gather.2.cloned.1.call-start = ((), (), s32[]{:S(2)}) async-start(), calls=%async_computation.2 | async-start | bytes 15728640 | tf_op jit(solution)/shard_map/all_gather | solution.py:17
  115.2 5.8 slice-start
  528.6 404.3 %all-to-all-start.1 = ((f32[1024,8,512]{2,0,1:T(8,128)}), f32[1024,8,512]{2,0,1:T(8,128)}, u32[]{:S(2)}, u32[]{:S(2)}) async-start(f32[1024,8,512]{2,0,1:T(8,128)} %rev.3), calls=%async_computation.1 | async-start | bytes 33554432 | tf_op jit(solution)/shard_map/all_to_all | solution.py:35
  554.1 372.9 %collective-permute-start = (bf16[768,1024]{1,0:T(8,128)(2,1)S(1)}, bf16[768,1024]{1,0:T(8,128)(2,1)S(1)}, u32[]{:S(2)}, u32[]{:S(2)}) collective-permute-start(bf16[768,1024]{1,0:T(8,128)(2,1)S(1)} %get-tuple-element.2), channel_id=1, source_target_pairs={{4,0},{8,4},{12,8},{16,12},{20,16},{24,20},{28,24},{5,1},{9,5},{13... | collective-permute-start | bytes 4718600 | tf_op jit(solution)/shard_map/ppermute | solution.py:10
  557.2 373.8 %collective-permute-start.1 = (bf16[768,1024]{1,0:T(8,128)(2,1)S(1)}, bf16[768,1024]{1,0:T(8,128)(2,1)S(1)}, u32[]{:S(2)}, u32[]{:S(2)}) collective-permute-start(bf16[768,1024]{1,0:T(8,128)(2,1)S(1)} %get-tuple-element.3), channel_id=1, source_target_pairs={{0,4},{4,8},{8,12},{12,16},{16,20},{20,24},{24,28},{1,5},{5,9},{9,... | collective-permute-start | bytes 4718600 | tf_op jit(solution)/shard_map/ppermute | solution.py:10
  950.6 33.3 %copy-start.1 = (bf16[1,2,768,1024]{3,2,1,0:T(8,128)(2,1)S(1)}, bf16[1,2,768,1024]{3,2,1,0:T(8,128)(2,1)}, u32[]{:S(2)}) copy-start(bf16[1,2,768,1024]{3,2,1,0:T(8,128)(2,1)} %param.4) | copy-start | bytes 9437188
Sparse Core Ops, SparseCore 0:
  9.6 83.5 all-gather.1
where the time goes:
time: 992 us; the launch traced here: 991 us
  waiting for transfers between devices  457 us (46%)
  blocking collectives  367 us (37%)
  local copies, waits for them, and re-layouts  83.2 us (8%)
  matrix products  40.6 us (4%)
  other arithmetic  16.9 us (2%)
  between operations  14.1 us (1%)
  starting transfers between devices  12 us (1%)
    ppermute x2, waiting for transfers between devices, from_behind(): return lax.ppermute(value, axis, pairs)  371 us
    all_to_all x1, blocking collectives, shards(): lax.all_to_all(blocked, 'pipe', split_axis=1, concat_axis=1, tiled=True)  367 us
    all_gather x1, waiting for transfers between devices, shards(): piece = lax.all_gather(grad_out, 'tensor', axis=2, tiled=True)  85.3 us
    dot_general x1, matrix products, shards(): jnp.einsum('rtd,rto->rdo', context_rows, piece[0, :owned], preferred_elem...  22 us
  transfers between devices with their start and end apart: 4, of which 3 were waited for; matrix products, arithmetic and copies ran while one was open for 2% of the time, Pallas kernels for 0%

commit v1 on v0

v1 whole, which is shorter than its diff:
```python
import jax
import jax.numpy as jnp
from jax import lax
from jax.sharding import PartitionSpec as P


def from_behind(value, axis, by):
    count = lax.axis_size(axis)
    pairs = [(i, i + by) for i in range(count) if 0 <= i + by < count]
    return lax.ppermute(value, axis, pairs)


def from_mirror(value, axis):
    count = lax.axis_size(axis)
    return lax.ppermute(value, axis, [(i, count - 1 - i) for i in range(count)])


def weight_part(rows, gradient):
    return jnp.einsum("td,to->do", rows, gradient, preferred_element_type=jnp.float32)


def back_part(gradient, weights):
    return jnp.einsum(
        "to,do->td", gradient, weights, preferred_element_type=jnp.float32
    ).astype(jnp.bfloat16)


def shards(section_weights, context, grad_out):
    far_grad = from_mirror(grad_out[0, 1], "pipe")
    far_context = from_mirror(context[0, 1], "pipe")
    up = lax.all_gather(grad_out[0, 1], "tensor", axis=0, tiled=True)
    down = lax.all_gather(grad_out[0, 0], "tensor", axis=0, tiled=True)
    from_prior = from_behind(back_part(up, section_weights[0, 1]), "pipe", 1)
    from_next = from_behind(back_part(down, section_weights[0, 0]), "pipe", -1)
    far = lax.all_gather(far_grad, "tensor", axis=0, tiled=True)
    total = weight_part(context[0, 0], down) + weight_part(far_context, far)
    weight_grad = total.astype(jnp.bfloat16)[None]
    input_grad = jnp.stack([from_next, from_prior])[None]
    return (weight_grad, input_grad)


def solution(mesh):
    placed = (
        P("pipe", None, "tensor", None),
        P("pipe", None, None, "tensor"),
        P("pipe", None, "tensor", None),
    )
    return jax.shard_map(
        shards,
        mesh=mesh,
        in_specs=placed,
        out_specs=(P("pipe", "tensor", None), P("pipe", None, None, "tensor")),
        check_vma=False,
    )
```

time: 992 us -> 246 us (0.25)
  blocking collectives: 367 us -> 0 us
  waiting for transfers between devices: 457 us -> 166 us
  local copies, waits for them, and re-layouts: 83.2 us -> 5.4 us
  other arithmetic: 16.9 us -> 3.36 us
    all_to_all x1 -> x0, blocking collectives: 367 us -> none  [shards(): lax.all_to_all(blocked, 'pipe', split_axis=1, concat_axis=1, tiled=True)]
    ppermute x2, waiting for transfers between devices: 371 us -> 67.5 us  [from_behind(): return lax.ppermute(value, axis, pairs)]
    ppermute x0 -> x2, waiting for transfers between devices: none -> 89.1 us  [from_mirror(): return lax.ppermute(value, axis, [(i, count - 1 - i) for i in range(count)])]
    all_gather x1 -> x3, waiting for transfers between devices: 85.3 us -> 8.96 us  [the longest x1 8.95 us: shards(): up = lax.all_gather(grad_out[0, 1], 'tensor', axis=0, tiled=True)]
    another operation x1 -> x0, local copies, waits for them, and re-layouts: 19 us -> none  [shards(): blocked = weight_sum[1].reshape(width_in, pieces, width_out // pieces)]
    reshape x1 -> x0, local copies, waits for them, and re-layouts: 18.3 us -> none  [shards(): lax.all_to_all(turned, 'pipe', split_axis=1, concat_axis=1, tiled=True)]
    all_to_all x1 -> x0, local copies, waits for them, and re-layouts: 17.7 us -> none  [shards(): lax.all_to_all(turned, 'pipe', split_axis=1, concat_axis=1, tiled=True)]
    convert_element_type x1 -> x0, other arithmetic: 14.9 us -> none  [shards(): weight_grad = (weight_sum[0] + partner).astype(jnp.bfloat16)[None]]
  transfers between devices with their start and end apart: 4 -> 7, of which waited for: 3 -> 5; matrix products, arithmetic and copies ran while one was open for 2% -> 15% of each run, Pallas kernels for 0% -> 0%
where the time goes in v1:
time: 246 us; the launch traced here: 245 us
  waiting for transfers between devices  166 us (67%)
  matrix products  47.4 us (19%)
  between operations  13.8 us (6%)
  starting transfers between devices  9.3 us (4%)
  local copies, waits for them, and re-layouts  5.4 us (2%)
  other arithmetic  3.36 us (1%)
    ppermute x2, waiting for transfers between devices, from_mirror(): return lax.ppermute(value, axis, [(i, count - 1 - i) for i in range(count)])  89.1 us
    ppermute x2, waiting for transfers between devices, from_behind(): return lax.ppermute(value, axis, pairs)  67.5 us
    dot_general x2, matrix products, weight_part(): jnp.einsum('td,to->do', rows, gradient, preferred_element_type=jnp.float32)  24.1 us
    dot_general x2, matrix products, back_part(): jnp.einsum('to,do->td', gradient, weights, preferred_element_type=jnp.flo...  23.3 us
    all_gather x1, waiting for transfers between devices, shards(): up = lax.all_gather(grad_out[0, 1], 'tensor', axis=0, tiled=True)  8.95 us
    ppermute x2, starting transfers between devices, from_behind(): return lax.ppermute(value, axis, pairs)  6.78 us
  transfers between devices with their start and end apart: 7, of which 5 were waited for; matrix products, arithmetic and copies ran while one was open for 15% of the time, Pallas kernels for 0%

profile of v1, /device:TPU:17, one launch (start us, length us, event | category | flops | bytes accessed | tf_op | source)
XLA Modules:
  0.0 245.4 jit_solution(6875355880374545605)
XLA Ops:
  7.2 0.0 all-gather.8.cloned.1.call-start
  7.2 4.1 %fusion.23 = (bf16[1,1,192,4096]{3,2,1,0:T(8,128)(2,1)}, bf16[192,4096]{1,0:T(8,128)(2,1)S(1)}, bf16[1,1,192,4096]{3,2,1,0:T(8,128)(2,1)}) fusion(bf16[1,2,192,4096]{3,2,1,0:T(8,128)(2,1)} %param.5), kind=kLoop, calls=%fused_computation.19 | loop fusion | bytes 7864320 | tf_op jit(solution)/shard_map/slice | solution.py:29
  11.3 0.0 all-gather.8.cloned.1.call-update
  11.4 0.0 all-gather.10.cloned.1.call-start
  11.4 0.7 all-gather.10.cloned.1.call-update
  12.1 0.0 all-gather.6.cloned.1.call-start
  12.2 1.2 collective-permute-start.1
  13.3 68.8 %collective-permute-done.1 = bf16[192,4096]{1,0:T(8,128)(2,1)S(1)} collective-permute-done((bf16[192,4096]{1,0:T(8,128)(2,1)S(1)}, bf16[192,4096]{1,0:T(8,128)(2,1)S(1)}, u32[]{:S(2)}, u32[]{:S(2)}) %collective-permute-start.1) | collective-permute-done | bytes 1572896 | tf_op jit(solution)/shard_map/ppermute | solution.py:15
  82.1 0.0 copy-start.2
  82.1 1.1 copy-done.2
  83.2 0.0 all-gather.6.cloned.1.call-update
  83.3 0.0 all-gather.8.cloned.1.call-done
  83.3 12.2 %fusion.11 = bf16[768,1024]{1,0:T(8,128)(2,1)} fusion(bf16[1,2,1024,4096]{3,2,1,0:T(8,128)(2,1)} %param.3, bf16[1,1,768,4096]{3,2,1,0:T(8,128)(2,1)} %all-gather.8.cloned.1.call-done), kind=kOutput, calls=%fused_computation.13 | convolution fusion | flops 6443237376 | bytes 16252928 | tf_op jit(solution)/shard_map/to,do->td/dot_general | solution.py:23
  95.5 0.0 copy-start.1
  95.5 3.5 %collective-permute-start.2 = (bf16[768,1024]{1,0:T(8,128)(2,1)}, bf16[768,1024]{1,0:T(8,128)(2,1)}, u32[]{:S(2)}, u32[]{:S(2)}) collective-permute-start(bf16[768,1024]{1,0:T(8,128)(2,1)} %fusion.11), channel_id=1, source_target_pairs={{4,0},{8,4},{12,8},{16,12},{20,16},{24,20},{28,24},{5,1},{9,5},{13... | collective-permute-start | bytes 4718600 | tf_op jit(solution)/shard_map/ppermute | solution.py:10
  99.0 8.9 %all-gather.10.cloned.1.call-done = bf16[1,1,768,4096]{3,2,1,0:T(8,128)(2,1)} async-done(((bf16[1,1,192,4096]{3,2,1,0:T(8,128)(2,1)}), bf16[1,1,768,4096]{3,2,1,0:T(8,128)(2,1)}) %all-gather.10.cloned.1.call-update) | async-done | bytes 6291472 | tf_op jit(solution)/shard_map/all_gather | solution.py:31
  107.9 0.0 copy-start
  107.9 11.1 %fusion.16 = bf16[768,1024]{1,0:T(8,128)(2,1)S(1)} fusion(bf16[1,2,1024,4096]{3,2,1,0:T(8,128)(2,1)} %param.3, bf16[1,1,768,4096]{3,2,1,0:T(8,128)(2,1)} %all-gather.10.cloned.1.call-done), kind=kOutput, calls=%fused_computation.14 | convolution fusion | flops 6443237376 | bytes 16252928 | tf_op jit(solution)/shard_map/to,do->td/dot_general | solution.py:23
  119.1 3.3 %collective-permute-start.3 = (bf16[768,1024]{1,0:T(8,128)(2,1)S(1)}, bf16[768,1024]{1,0:T(8,128)(2,1)S(1)}, u32[]{:S(2)}, u32[]{:S(2)}) collective-permute-start(bf16[768,1024]{1,0:T(8,128)(2,1)S(1)} %fusion.16), channel_id=1, source_target_pairs={{0,4},{4,8},{8,12},{12,16},{16,20},{20,24},{24,28},{1,5},{5,9},{9,... | collective-permute-start | bytes 4718600 | tf_op jit(solution)/shard_map/ppermute | solution.py:10
  122.3 0.0 copy-done.1
  122.4 0.1 slice_bitcast_fusion
  122.5 1.2 collective-permute-start
  123.7 0.0 copy-done
  123.7 10.3 %fusion.9 = f32[1024,4096]{1,0:T(8,128)} fusion(bf16[1,1,768,4096]{3,2,1,0:T(8,128)(2,1)S(1)} %copy-done, bf16[1,2,768,1024]{3,2,1,0:T(8,128)(2,1)S(1)} %copy-done.1), kind=kOutput, calls=%fused_computation.10 | convolution fusion | flops 6442450944 | bytes 24641536 | tf_op jit(solution)/shard_map/td,to->do/dot_general | solution.py:19
  134.1 33.1 %collective-permute-done.2 = bf16[768,1024]{1,0:T(8,128)(2,1)} collective-permute-done((bf16[768,1024]{1,0:T(8,128)(2,1)}, bf16[768,1024]{1,0:T(8,128)(2,1)}, u32[]{:S(2)}, u32[]{:S(2)}) %collective-permute-start.2) | collective-permute-done | bytes 1572896 | tf_op jit(solution)/shard_map/ppermute | solution.py:10
  167.2 34.4 %collective-permute-done.3 = bf16[768,1024]{1,0:T(8,128)(2,1)S(1)} collective-permute-done((bf16[768,1024]{1,0:T(8,128)(2,1)S(1)}, bf16[768,1024]{1,0:T(8,128)(2,1)S(1)}, u32[]{:S(2)}, u32[]{:S(2)}) %collective-permute-start.3) | collective-permute-done | bytes 1572896 | tf_op jit(solution)/shard_map/ppermute | solution.py:10
  201.5 3.4 %maximum_bitcast_fusion = bf16[1,2,768,1024]{3,2,1,0:T(8,128)(2,1)} fusion(bf16[1,768,1024]{2,1,0:T(8,128)(2,1)S(1)} %bitcast.37, bf16[1,768,1024]{2,1,0:T(8,128)(2,1)} %bitcast.6), kind=kLoop, calls=%fused_computation.12 | loop fusion | flops 1572864 | bytes 6291456 | tf_op jit(solution)/shard_map/broadcast_in_dim | solution.py:38
  204.9 20.3 %collective-permute-done = bf16[768,1024]{1,0:T(8,128)(2,1)} collective-permute-done((bf16[768,1024]{1,0:T(8,128)(2,1)S(1)}, bf16[768,1024]{1,0:T(8,128)(2,1)}, u32[]{:S(2)}, u32[]{:S(2)}) %collective-permute-start) | collective-permute-done | bytes 1572896 | tf_op jit(solution)/shard_map/ppermute | solution.py:15
  225.2 0.0 all-gather.6.cloned.1.call-done
  225.2 13.8 %fusion = bf16[1,1024,4096]{2,1,0:T(8,128)(2,1)} fusion(f32[1024,4096]{1,0:T(8,128)} %fusion.9, bf16[768,1024]{1,0:T(8,128)(2,1)} %collective-permute-done, bf16[768,4096]{1,0:T(8,128)(2,1)} %all-gather.6.cloned.1.call-done), kind=kOutput, calls=%fused_computation.1 | convolution fusion | flops 6450839552 | bytes 33030144 | tf_op jit(solution)/shard_map/td,to->do/dot_general | solution.py:19
Async XLA Ops:
  7.2 76.1 %all-gather.8.cloned.1.call-start = ((), (), s32[]{:S(2)}) async-start(), calls=%async_computation.1 | async-start | bytes 7864320 | tf_op jit(solution)/shard_map/all_gather | solution.py:32
  11.4 96.6 %all-gather.10.cloned.1.call-start = ((), (), s32[]{:S(2)}) async-start(), calls=%async_computation.2 | async-start | bytes 7864320 | tf_op jit(solution)/shard_map/all_gather | solution.py:31
  12.1 213.1 %all-gather.6.cloned.1.call-start = ((), (), s32[]{:S(2)}) async-start(), calls=%async_computation | async-start | bytes 7864320 | tf_op jit(solution)/shard_map/all_gather | solution.py:35
  12.2 69.9 %collective-permute-start.1 = (bf16[192,4096]{1,0:T(8,128)(2,1)S(1)}, bf16[192,4096]{1,0:T(8,128)(2,1)S(1)}, u32[]{:S(2)}, u32[]{:S(2)}) collective-permute-start(bf16[192,4096]{1,0:T(8,128)(2,1)S(1)} %get-tuple-element.3), channel_id=1, source_target_pairs={{0,28},{4,24},{8,20},{12,16},{16,12},{20,8},{24,4},{28,0},{1,29},{... | collective-permute-start | bytes 4718600 | tf_op jit(solution)/shard_map/ppermute | solution.py:15
  82.1 1.1 copy-start.2
  95.5 26.9 %copy-start.1 = (bf16[1,2,768,1024]{3,2,1,0:T(8,128)(2,1)S(1)}, bf16[1,2,768,1024]{3,2,1,0:T(8,128)(2,1)}, u32[]{:S(2)}) copy-start(bf16[1,2,768,1024]{3,2,1,0:T(8,128)(2,1)} %param.4) | copy-start | bytes 9437188
  95.5 71.7 %collective-permute-start.2 = (bf16[768,1024]{1,0:T(8,128)(2,1)}, bf16[768,1024]{1,0:T(8,128)(2,1)}, u32[]{:S(2)}, u32[]{:S(2)}) collective-permute-start(bf16[768,1024]{1,0:T(8,128)(2,1)} %fusion.11), channel_id=1, source_target_pairs={{4,0},{8,4},{12,8},{16,12},{20,16},{24,20},{28,24},{5,1},{9,5},{13... | collective-permute-start | bytes 4718600 | tf_op jit(solution)/shard_map/ppermute | solution.py:10
  107.9 15.8 %copy-start = (bf16[1,1,768,4096]{3,2,1,0:T(8,128)(2,1)S(1)}, bf16[1,1,768,4096]{3,2,1,0:T(8,128)(2,1)}, u32[]{:S(2)}) copy-start(bf16[1,1,768,4096]{3,2,1,0:T(8,128)(2,1)} %all-gather.8.cloned.1.call-done) | copy-start | bytes 18874372
  119.1 82.5 %collective-permute-start.3 = (bf16[768,1024]{1,0:T(8,128)(2,1)S(1)}, bf16[768,1024]{1,0:T(8,128)(2,1)S(1)}, u32[]{:S(2)}, u32[]{:S(2)}) collective-permute-start(bf16[768,1024]{1,0:T(8,128)(2,1)S(1)} %fusion.16), channel_id=1, source_target_pairs={{0,4},{4,8},{8,12},{12,16},{16,20},{20,24},{24,28},{1,5},{5,9},{9,... | collective-permute-start | bytes 4718600 | tf_op jit(solution)/shard_map/ppermute | solution.py:10
  122.5 102.7 %collective-permute-start = (bf16[768,1024]{1,0:T(8,128)(2,1)S(1)}, bf16[768,1024]{1,0:T(8,128)(2,1)}, u32[]{:S(2)}, u32[]{:S(2)}) collective-permute-start(bf16[768,1024]{1,0:T(8,128)(2,1)S(1)} %slice_bitcast_fusion), channel_id=1, source_target_pairs={{0,28},{4,24},{8,20},{12,16},{16,12},{20,8},{24,4},{28,0},{1,29},{... | collective-permute-start | bytes 4718600 | tf_op jit(solution)/shard_map/ppermute | solution.py:15
Sparse Core Ops, SparseCore 0:
  11.5 47.8 all-gather.7
  61.5 46.3 all-gather.9
  109.5 46.3 all-gather.5

commit v2 on v1

v2 whole, which is shorter than its diff:
```python
import functools

import jax
import jax.numpy as jnp
from jax import lax
from jax.experimental import pallas as pl
from jax.experimental.pallas import tpu as pltpu
from jax.sharding import PartitionSpec as P

MESH = pl.DeviceIdType.MESH
UP, DOWN, FAR = 1, 0, 2


def flip(index, bit):
    return index + bit - 2 * bit * ((index // bit) % 2)


def kernel(
    pipes, group, w_ref, c_ref, g_ref, wg_ref, ig_ref,
    grads, weights, context, far_context, back, turned, total,
    gather_send, gather_recv, far_send, far_recv, column_send, column_recv,
    relay_send, relay_recv, own_sem, load_sem, zero_sem, store_sem,
):
    p = lax.axis_index("pipe")
    t = lax.axis_index("tensor")
    mirror = pipes - 1 - p
    share = g_ref.shape[2]
    tokens, width_out = grads.shape[1:]
    width_in = weights.shape[0]
    block = turned.shape[0]
    blocks = width_in // block
    bits = []
    while (group >> (len(bits) + 1)) > 0:
        bits.append(group >> (len(bits) + 1))
    has_prior, has_next = p > 0, p < pipes - 1

    def piece_rows(piece):
        return pl.ds(pl.multiple_of(piece * share, 16), share)

    def gather_copies(stream, level):
        partner = flip(t, bits[level])
        copies = []
        for m in range(1 << level):
            piece = t
            for j in range(level):
                if (m >> j) & 1:
                    piece = flip(piece, bits[j])
            k = (1 << level) - 1 + m
            rows = piece_rows(piece)
            source = grads.at[stream, rows]
            if m == 0 and stream != FAR:
                source = g_ref.at[0, stream]
            copies.append(
                pltpu.make_async_remote_copy(
                    src_ref=source,
                    dst_ref=grads.at[stream, rows],
                    send_sem=gather_send.at[stream, k],
                    recv_sem=gather_recv.at[stream, k],
                    device_id=(p, partner),
                    device_id_type=MESH,
                )
            )
        return copies

    def gather_wait(stream, level):
        partner = flip(t, bits[level])
        for m in range(1 << level):
            piece = partner
            for j in range(level):
                if (m >> j) & 1:
                    piece = flip(piece, bits[j])
            k = (1 << level) - 1 + m
            rows = piece_rows(piece)
            pltpu.make_async_remote_copy(
                src_ref=grads.at[stream, rows],
                dst_ref=grads.at[stream, rows],
                send_sem=gather_send.at[stream, k],
                recv_sem=gather_recv.at[stream, k],
                device_id=(p, partner),
                device_id_type=MESH,
            ).wait_recv()

    far_copy = pltpu.make_async_remote_copy(
        src_ref=g_ref.at[0, UP],
        dst_ref=grads.at[FAR, piece_rows(t)],
        send_sem=far_send.at[0],
        recv_sem=far_recv.at[0],
        device_id=(mirror, t),
        device_id_type=MESH,
    )

    def column_copy(c):
        columns = pl.ds(c * block, block)
        return pltpu.make_async_remote_copy(
            src_ref=c_ref.at[0, UP, :, columns],
            dst_ref=far_context.at[:, columns],
            send_sem=column_send.at[c],
            recv_sem=column_recv.at[c],
            device_id=(mirror, t),
            device_id_type=MESH,
        )

    def relay(replica, to):
        return pltpu.make_async_remote_copy(
            src_ref=back.at[replica],
            dst_ref=ig_ref.at[0, replica],
            send_sem=relay_send.at[replica],
            recv_sem=relay_recv.at[replica],
            device_id=(to, t),
            device_id_type=MESH,
        )

    def load_weights(replica):
        return pltpu.make_async_copy(w_ref.at[0, replica], weights, load_sem.at[0])

    def zero(replica):
        return pltpu.make_async_copy(back.at[replica], ig_ref.at[0, 1 - replica], zero_sem.at[0])

    def multiply_back(replica):
        half = tokens // 2

        @pl.loop(0, blocks)
        def _(c):
            columns = pl.ds(pl.multiple_of(c * block, block), block)

            @pl.loop(0, 2)
            def _(h):
                rows = pl.ds(pl.multiple_of(h * half, half), half)
                product = lax.dot_general(
                    grads[replica, rows, :], weights[columns, :],
                    (((1,), (1,)), ((), ())), preferred_element_type=jnp.float32,
                )
                back[replica, rows, columns] = product.astype(back.dtype)

    slab = 512
    slabs = width_out // slab

    own = [
        pltpu.make_async_copy(g_ref.at[0, r], grads.at[r, piece_rows(t)], own_sem.at[r])
        for r in (0, 1)
    ]
    load_context = pltpu.make_async_copy(c_ref.at[0, DOWN], context, load_sem.at[1])

    barrier = pltpu.get_barrier_semaphore()
    pl.semaphore_signal(barrier, inc=1, device_id=(mirror, t), device_id_type=MESH)
    for bit in bits:
        pl.semaphore_signal(barrier, inc=1, device_id=(p, flip(t, bit)), device_id_type=MESH)

    for beside in (lax.rem(p + 1, pipes), lax.rem(p + pipes - 1, pipes)):
        pl.semaphore_signal(barrier, inc=1, device_id=(beside, t), device_id_type=MESH)

    own[UP].start()
    own[DOWN].start()
    load_weights(UP).start()
    load_context.start()
    pl.semaphore_wait(barrier, 3 + len(bits))

    far_copy.start()
    gathers = {(s, l): gather_copies(s, l) for s in range(3) for l in range(len(bits))}
    gathers[UP, 0][0].start()
    for level in range(1, len(bits)):
        gathers[UP, level][0].start()
        gathers[DOWN, level][0].start()

    def finish_gather(stream):
        for level in range(len(bits)):
            gather_wait(stream, level)
            if level + 1 < len(bits):
                for later in range(level + 1, len(bits)):
                    for m in range(1 << level, 1 << (level + 1)):
                        gathers[stream, later][m].start()

    gathers[UP, 0][0].wait_send()
    gathers[DOWN, 0][0].start()
    finish_gather(UP)
    own[UP].wait()
    load_weights(UP).wait()
    multiply_back(UP)
    load_weights(DOWN).start()
    far_copy.wait_send()
    for c in range(blocks):
        column_copy(c).start()

    @pl.when(has_next)
    def _():
        relay(UP, p + 1).start()

    @pl.when(p == pipes - 1)
    def _():
        back[UP] = jnp.zeros(back.shape[1:], back.dtype)
        zero(UP).start()

    finish_gather(DOWN)
    own[DOWN].wait()
    far_copy.wait_recv()
    for level in range(len(bits)):
        gathers[FAR, level][0].start()

    load_weights(DOWN).wait()
    multiply_back(DOWN)

    @pl.when(has_prior)
    def _():
        relay(DOWN, p - 1).start()

    @pl.when(p == 0)
    def _():
        back[DOWN] = jnp.zeros(back.shape[1:], back.dtype)
        zero(DOWN).start()

    load_context.wait()

    @pl.loop(0, blocks)
    def _(c):
        columns = pl.ds(pl.multiple_of(c * block, block), block)
        turned[...] = context[:, columns].T

        @pl.loop(0, slabs)
        def _(n):
            part = pl.ds(pl.multiple_of(n * slab, slab), slab)
            total[columns, part] = jnp.dot(
                turned[...], grads[DOWN, :, part], preferred_element_type=jnp.float32
            )

    finish_gather(FAR)
    stores = []
    for c in range(blocks):
        column_copy(c).wait_recv()
        columns = pl.ds(c * block, block)
        turned[...] = far_context[:, columns].T

        @pl.loop(0, slabs)
        def _(n):
            part = pl.ds(pl.multiple_of(n * slab, slab), slab)
            weights[columns, part] = (
                total[columns, part]
                + jnp.dot(turned[...], grads[FAR, :, part], preferred_element_type=jnp.float32)
            ).astype(weights.dtype)

        store = pltpu.make_async_copy(
            weights.at[columns], wg_ref.at[0, columns], store_sem.at[c]
        )
        store.start()
        stores.append(store)

    for store in stores:
        store.wait()
    far_copy_done = [gathers[UP, l][m] for l in range(1, len(bits)) for m in range(1 << l)]
    far_copy_done += [gathers[s, l][m] for s in (DOWN, FAR) for l in range(len(bits)) for m in range(1 << l)]
    far_copy_done += [column_copy(c) for c in range(blocks)]
    for copy in far_copy_done:
        copy.wait_send()

    @pl.when(has_next)
    def _():
        relay(UP, p + 1).wait_send()
        relay(DOWN, p + 1).wait_recv()

    @pl.when(has_prior)
    def _():
        relay(DOWN, p - 1).wait_send()
        relay(UP, p - 1).wait_recv()

    @pl.when(p == pipes - 1)
    def _():
        zero(UP).wait()

    @pl.when(p == 0)
    def _():
        zero(DOWN).wait()


def shards(pipes, group, section_weights, context, grad_out):
    width_in, width_out = section_weights.shape[2:]
    tokens = context.shape[2]
    block = min(256, width_in)
    blocks = width_in // block
    kind = jnp.bfloat16
    dma = pltpu.SemaphoreType.DMA
    anywhere = pl.BlockSpec(memory_space=pl.ANY)
    return pl.pallas_call(
        functools.partial(kernel, pipes, group),
        out_shape=(
            jax.ShapeDtypeStruct((1, width_in, width_out), kind),
            jax.ShapeDtypeStruct((1, 2, tokens, width_in), kind),
        ),
        in_specs=[anywhere] * 3,
        out_specs=(anywhere, anywhere),
        scratch_shapes=[
            pltpu.VMEM((3, tokens, width_out), kind),
            pltpu.VMEM((width_in, width_out), kind),
            pltpu.VMEM((tokens, width_in), kind),
            pltpu.VMEM((tokens, width_in), kind),
            pltpu.VMEM((2, tokens, width_in), kind),
            pltpu.VMEM((block, tokens), kind),
            pltpu.VMEM((width_in, width_out), jnp.float32),
            dma((3, group - 1)),
            dma((3, group - 1)),
            dma((1,)),
            dma((1,)),
            dma((blocks,)),
            dma((blocks,)),
            dma((2,)),
            dma((2,)),
            dma((2,)),
            dma((2,)),
            dma((1,)),
            dma((blocks,)),
        ],
        compiler_params=pltpu.CompilerParams(
            collective_id=0, has_side_effects=True, vmem_limit_bytes=58 * 2**20
        ),
        cost_estimate=pl.CostEstimate(
            flops=8 * tokens * width_in * width_out,
            bytes_accessed=2 * (3 * width_in * width_out + 9 * tokens * width_in),
            transcendentals=0,
        ),
    )(section_weights, context, grad_out)


def solution(mesh):
    placed = (
        P("pipe", None, "tensor", None),
        P("pipe", None, None, "tensor"),
        P("pipe", None, "tensor", None),
    )
    return jax.shard_map(
        functools.partial(shards, mesh.shape["pipe"], mesh.shape["tensor"]),
        mesh=mesh,
        in_specs=placed,
        out_specs=(P("pipe", "tensor", None), P("pipe", None, None, "tensor")),
        check_vma=False,
    )
```

time: 246 us -> 218 us (0.89)
  Pallas kernels: 0 us -> 207 us
  waiting for transfers between devices: 166 us -> 0 us
  matrix products: 47.4 us -> 0 us
  between operations: 13.8 us -> 0.65 us
  starting transfers between devices: 9.3 us -> 0 us
  local copies, waits for them, and re-layouts: 5.4 us -> 9.71 us
  other arithmetic: 3.36 us -> 0 us
    pallas_call x0 -> x1, Pallas kernels: none -> 207 us  [shards(): pl.pallas_call(functools.partial(kernel, pipes, group), out_shape=(jax.Sh...]
    ppermute x4 -> x0, waiting for transfers between devices: 157 us -> none  [the longest x2 89.1 us: from_mirror(): return lax.ppermute(value, axis, [(i, count - 1 - i) for i in range(count)])]
    dot_general x4 -> x0, matrix products: 47.4 us -> none  [the longest x2 24.1 us: weight_part(): jnp.einsum('td,to->do', rows, gradient, preferred_element_type=jnp.float32)]
    ppermute x4 -> x0, starting transfers between devices: 9.18 us -> none  [the longest x2 6.78 us: from_behind(): return lax.ppermute(value, axis, pairs)]
    all_gather x3 -> x0, waiting for transfers between devices: 8.96 us -> none  [the longest x1 8.95 us: shards(): up = lax.all_gather(grad_out[0, 1], 'tensor', axis=0, tiled=True)]
    unnamed x6 -> x4, local copies, waits for them, and re-layouts: 1.16 us -> 9.71 us
    slice x1 -> x0, local copies, waits for them, and re-layouts: 4.12 us -> none  [shards(): far_grad = from_mirror(grad_out[0, 1], 'pipe')]
    broadcast_in_dim x1 -> x0, other arithmetic: 3.36 us -> none  [shards(): input_grad = jnp.stack([from_next, from_prior])[None]]
  transfers between devices with their start and end apart: 7 -> 0, of which waited for: 5 -> 0; matrix products, arithmetic and copies ran while one was open for 15% -> 0% of each run, Pallas kernels for 0% -> 0%
where the time goes in v2:
time: 218 us; the launch traced here: 217 us
  Pallas kernels  207 us (95%)
  local copies, waits for them, and re-layouts  9.71 us (4%)
    pallas_call x1, Pallas kernels, shards(): pl.pallas_call(functools.partial(kernel, pipes, group), out_shape=(jax.Sh...  207 us
    unnamed x4, local copies, waits for them, and re-layouts  9.71 us

profile of v2, /device:TPU:17, one launch (start us, length us, event | category | flops | bytes accessed | tf_op | source)
XLA Modules:
  0.0 216.9 jit_solution(5815218552054314662)
XLA Ops:
  0.6 206.6 %shard_map.50 = (bf16[1,1024,4096]{2,1,0:T(8,128)(2,1)}, bf16[1,2,768,1024]{3,2,1,0:T(8,128)(2,1)}) custom-call(bf16[1,2,1024,4096]{3,2,1,0:T(8,128)(2,1)} %w_ref.1, bf16[1,2,768,1024]{3,2,1,0:T(8,128)(2,1)} %c_ref.1, bf16[1,2,192,4096]{3,2,1,0:T(8,128)(2,1)} %g_ref.1), custom_call_target="tpu_custom_call" | custom-call | flops 25769803776 | bytes 39321600 | tf_op jit(solution)/shard_map/pallas_call | solution.py:281
  207.2 0.0 copy-start
  207.2 8.0 %copy.7 = bf16[1,1024,4096]{2,1,0:T(8,128)(2,1)} copy(bf16[1,1024,4096]{2,1,0:T(8,128)(2,1)} %get-tuple-element.4) | data formatting | bytes 16777216
  215.2 0.0 copy-done
  215.2 1.7 copy.8
Async XLA Ops:
  207.2 8.1 %copy-start = (bf16[1,2,768,1024]{3,2,1,0:T(8,128)(2,1)S(1)}, bf16[1,2,768,1024]{3,2,1,0:T(8,128)(2,1)}, u32[]{:S(2)}) copy-start(bf16[1,2,768,1024]{3,2,1,0:T(8,128)(2,1)} %get-tuple-element.5) | copy-start | bytes 9437188
